TPU v7x, 32 devices: a whole 2x2x4 slice. The times are simulated.
32 devices in a mesh: sta: 16 (over z, y, x), pt: 2 (over core).
Axes of the slice: x: 2, y: 2, z: 4, core: 2. Of those that a mesh axis runs over, the one named last changes fastest.
Arguments:
- greens: bfloat16 [2, 64, 1024], P(None, 'sta', 'pt'), may hold values from -6 to 6
- source_power: float32 [1024], P('pt'), may hold values from 0.25 to 4
- observed: float32 [2, 64, 64], P(None, 'sta'), may hold values from -6 to 6
- pair_class: int32 [64, 64], P('sta'), may hold values from 0 to 7
- class_weight: float32 [8], replicated, may hold values from 0.5 to 4
Outputs:
- correlations: float32 [2, 64, 64], P(None, 'sta', 'pt')
- source_gradient: float32 [1024], P('pt')
All inputs are finite; a program needn't handle non-finite values.
Results may differ from a plain program's by a relative error of at most 0.0018.
Values may be sent and summed in bfloat16 or wider, within the bound.
A program may use at most 64 MiB of HBM per device.

v0:
```python
import math

import jax
import jax.numpy as jnp
from jax import lax
from jax.sharding import PartitionSpec as P

CLASSES = 8


def last_dot(left, right):
    return lax.dot_general(
        left, right, (((1,), (1,)), ((), ())), preferred_element_type=jnp.float32
    )


def pair_weights(classes, class_weight, row_first):
    total = jnp.zeros(classes.shape, jnp.float32)
    for level in range(1, CLASSES):
        total = total + jnp.where(classes == level, class_weight[level], 0.0)
    row_ids = row_first + jnp.arange(classes.shape[0], dtype=jnp.int32)[:, None]
    col_ids = jnp.arange(classes.shape[1], dtype=jnp.int32)[None, :]
    return jnp.where(row_ids == col_ids, 0.0, total)


def body(greens, source_power, observed, pair_class, class_weight):
    own_rows = greens.shape[1]
    local_pts = greens.shape[2]
    sta_count = lax.axis_size("sta")
    pt_count = lax.axis_size("pt")
    all_stations = own_rows * sta_count
    scale_pts = 1.0 / math.sqrt(local_pts * pt_count)
    weighted = (source_power[None, None, :] * greens.astype(jnp.float32)).astype(jnp.bfloat16)
    row_first = lax.axis_index("sta") * own_rows

    def make_field(adjoint):

        def add_field(running, shard_rows, first_row):
            part_real = jnp.dot(
                adjoint[0], shard_rows[0], preferred_element_type=jnp.float32
            ) + jnp.dot(adjoint[1], shard_rows[1], preferred_element_type=jnp.float32)
            part_imag = jnp.dot(
                adjoint[0], shard_rows[1], preferred_element_type=jnp.float32
            ) - jnp.dot(adjoint[1], shard_rows[0], preferred_element_type=jnp.float32)
            return jnp.stack([part_real, part_imag])

        return add_field

    shard_rows = lax.all_gather(greens, "sta", axis=1, tiled=True)
    block_real = last_dot(weighted[0], shard_rows[0]) + last_dot(weighted[1], shard_rows[1])
    block_imag = last_dot(weighted[0], shard_rows[1]) - last_dot(weighted[1], shard_rows[0])
    block = jnp.stack([block_real, block_imag])
    share_cols = all_stations // pt_count
    col_first = lax.axis_index("pt") * share_cols
    corr_full = lax.psum(block, "pt") * scale_pts
    weights = pair_weights(pair_class, class_weight, row_first)
    adjoint = (weights[None] * (corr_full - observed)).astype(jnp.bfloat16)
    corr_share = lax.dynamic_slice_in_dim(corr_full, col_first, share_cols, 2)
    field_empty = jnp.zeros((2, own_rows, local_pts), jnp.float32)
    add_field = make_field(adjoint)
    field = add_field(field_empty, lax.all_gather(greens, "sta", axis=1, tiled=True), jnp.int32(0))
    local_terms = jnp.sum(
        greens[0].astype(jnp.float32) * field[0] + greens[1].astype(jnp.float32) * field[1], axis=0
    )
    gradient = lax.psum(local_terms, "sta") / all_stations
    return (corr_share, gradient)


def solution(mesh):
    return jax.shard_map(
        body,
        mesh=mesh,
        in_specs=(P(None, "sta", "pt"), P("pt"), P(None, "sta", None), P("sta", None), P()),
        out_specs=(P(None, "sta", "pt"), P("pt")),
        check_vma=False,
    )
```

profile of v0, /device:TPU:0, one launch (start us, length us, event | category | flops | bytes accessed | tf_op | source)
XLA Modules:
  0.0 92.8 jit_solution(3078751469226195705)
XLA Ops:
  0.6 1.6 %fusion.11 = (f32[1]{0:T(128)}, f32[1]{0:T(128)}, f32[1]{0:T(128)}, f32[1]{0:T(128)}, f32[1]{0:T(128)}, /*index=5*/f32[1]{0:T(128)}, f32[1]{0:T(128)}) fusion(f32[8]{0:T(128)} %param.9), kind=kLoop, calls=%fused_computation.30 | loop fusion | bytes 56 | tf_op jit(solution)/shard_map/slice | solution.py:20
  2.2 0.0 copy-start.3
  2.2 0.0 copy-start
  2.2 0.7 copy-done.3
  2.9 4.5 %add_select_fusion = f32[4,64]{1,0:T(4,128)S(1)} fusion(s32[4,64]{1,0:T(4,128)S(1)} %copy-done.3, f32[]{:T(128)} %bitcast.13, f32[]{:T(128)} %bitcast.12, f32[]{:T(128)} %bitcast.11, f32[]{:T(128)} %bitcast.10, f32[]{:T(128)} %bitcast.9, f32[]{:T(128)} %bitcast.8, f32[]{:T(128)} %bitcast.7, s32[4]{0:T(128)S(1)} %iota_add_fusion), kind=kLoop, calls=%fused_computation.19 | loop fusion | flops 5632 | bytes 2092 | tf_op jit(solution)/shard_map/jit(_where)/select_n | solution.py:23
  7.4 0.0 copy-done
  7.4 43.1 %all_gather.4 = bf16[2,64,512]{2,0,1:T(2,128)(2,1)S(1)} all-gather(bf16[2,4,512]{2,0,1:T(2,128)(2,1)S(1)} %copy.8), channel_id=1, replica_groups=mesh['sta'=16,'pt'=2] {'sta'}, dimensions={1}, use_global_device_ids=true | all-gather | bytes 139264 | tf_op jit(solution)/shard_map/all_gather | solution.py:49
  50.5 0.2 fusion.10
  50.7 0.0 copy-start.2
  50.7 0.6 copy-done.2
  51.3 0.1 fusion.7
  51.5 0.1 fusion.5
  51.6 0.1 fusion.6
  51.7 0.1 fusion.4
  51.9 0.0 copy-start.1
  51.9 2.6 %psum.14 = f32[2,4,64]{2,1,0:T(4,128)S(1)} all-reduce(f32[2,4,64]{2,1,0:T(4,128)S(1)} %pad_maximum_fusion), channel_id=1, replica_groups=mesh['sta'=16,'pt'=2] {'pt'}, use_global_device_ids=true, to_apply=%region_0.0 | all-reduce | flops 512 | bytes 4096 | tf_op jit(solution)/shard_map/psum | solution.py:55
  54.5 0.0 copy-done.1
  54.5 0.1 fusion.8
  54.6 0.1 fusion.9
  54.7 0.1 fusion.2
  54.9 0.1 fusion.3
  55.0 36.6 %psum.15 = f32[512]{0:T(512)S(1)} all-reduce(f32[512]{0:T(512)S(1)} %fusion.3), channel_id=1, replica_groups=mesh['sta'=16,'pt'=2] {'sta'}, use_global_device_ids=true, to_apply=%region_2.3 | all-reduce | flops 512 | bytes 4096 | tf_op jit(solution)/shard_map/psum | solution.py:65
  91.6 0.6 broadcast_multiply_fusion.1
  92.1 0.7 constant_dynamic-slice_fusion
  (6 shorter events, 0.1 us)
Async XLA Ops:
  2.2 0.7 copy-start.3
  2.2 5.2 %copy-start = (bf16[2,4,512]{2,1,0:T(4,128)(2,1)S(1)}, bf16[2,4,512]{2,1,0:T(4,128)(2,1)}, u32[]{:S(2)}) copy-start(bf16[2,4,512]{2,1,0:T(4,128)(2,1)} %param.5) | copy-start | bytes 24580
  50.7 0.7 copy-start.2
  51.9 2.6 %copy-start.1 = (f32[2,4,64]{2,1,0:T(4,128)S(1)}, f32[2,4,64]{2,1,0:T(4,128)}, u32[]{:S(2)}) copy-start(f32[2,4,64]{2,1,0:T(4,128)} %param.7) | copy-start | bytes 6148
where the time goes:
time: 93.1 us; the launch traced here: 92.8 us
  blocking collectives  82.2 us (88%)
  other arithmetic  5.09 us (5%)
  local copies, waits for them, and re-layouts  3.79 us (4%)
  matrix products  1.02 us (1%)
    all_gather x1, blocking collectives, body(): shard_rows = lax.all_gather(greens, 'sta', axis=1, tiled=True)  43.1 us
    psum x1, blocking collectives, body(): gradient = lax.psum(local_terms, 'sta') / all_stations  36.6 us
    select_n x1, other arithmetic, pair_weights(): return jnp.where(row_ids == col_ids, 0.0, total)  4.48 us
    psum x1, blocking collectives, body(): corr_full = lax.psum(block, 'pt') * scale_pts  2.6 us

commit v1 on v0

v1 whole, which is shorter than its diff:
```python
import functools
import math

import jax
import jax.numpy as jnp
from jax import lax
from jax.experimental import pallas as pl
from jax.experimental.pallas import tpu as pltpu
from jax.sharding import PartitionSpec as P

CLASSES = 8
MESH = pl.DeviceIdType.MESH
UNROLL = 16


def each(first, last, step):
    if last - first <= UNROLL:
        for i in range(first, last):
            step(i)
    else:
        pl.loop(first, last)(step)


def kernel(
    n, m, greens_ref, power_ref, observed_ref, class_ref, weight_ref, corr_ref, grad_ref,
    greens_v, power_v, observed_v, class_v, weight_s, all_v, field_v, part_v, recv_v, gap_v, pair_v,
    in_sem, send_sem, recv_sem, pt_send, pt_recv,
):
    me, mine = lax.axis_index("sta"), lax.axis_index("pt")
    own, pts = greens_ref.shape[1], greens_ref.shape[2]
    stations = own * n
    half = pts // 2
    rows = 4 * own

    loads = [
        pltpu.make_async_copy(src, dst, in_sem.at[i])
        for i, (src, dst) in enumerate(
            ((greens_ref, greens_v), (observed_ref, observed_v), (class_ref, class_v),
             (power_ref, power_v), (weight_ref, weight_s))
        )
    ]
    for load in loads:
        load.start()

    barrier = pltpu.get_barrier_semaphore()

    def greet(i):
        pl.semaphore_signal(barrier, inc=1, device_id={"sta": lax.rem(me + i, n), "pt": mine}, device_id_type=MESH)

    def greet_pt(i):
        pl.semaphore_signal(barrier, inc=1, device_id={"sta": me, "pt": lax.rem(mine + i, m)}, device_id_type=MESH)

    each(1, n, greet)
    each(1, m, greet_pt)

    for load in loads[:3]:
        load.wait()
    g = greens_v[...].astype(jnp.float32)
    points = jnp.concatenate(
        [g[0, :, :half], g[1, :, :half], g[0, :, half:], g[1, :, half:]], axis=0
    ).astype(jnp.bfloat16)
    obs = jnp.concatenate([observed_v[0], observed_v[1]], axis=1)
    high = obs.astype(jnp.bfloat16).astype(jnp.float32)
    rest = obs - high
    mid = rest.astype(jnp.bfloat16).astype(jnp.float32)
    low = rest - mid
    cls = class_v[...].astype(jnp.float32)
    side = jnp.concatenate([high, mid, low, jnp.concatenate([cls, cls], axis=1)], axis=0).astype(jnp.bfloat16)
    here = all_v.at[pl.ds(pl.multiple_of(me * rows, rows), rows)]
    here[:, :half] = points
    here[:, half:] = side

    pl.semaphore_wait(barrier, (n - 1) + (m - 1))

    def send(i):
        pltpu.make_async_remote_copy(
            src_ref=here, dst_ref=here, send_sem=send_sem, recv_sem=recv_sem,
            device_id={"sta": lax.rem(me + i, n), "pt": mine}, device_id_type=MESH,
        ).start()

    each(1, n, send)

    group = math.gcd(n, 16)
    span = group * own
    size = group * rows
    at = lax.broadcasted_iota(jnp.int32, (size, size), 0)
    of = lax.broadcasted_iota(jnp.int32, (size, size), 1)
    source = (at % span) // own * rows + at // span * own + at % own
    order = jnp.where(of == source, 1.0, 0.0).astype(jnp.bfloat16)
    loads[3].wait()
    loads[4].wait()
    power = [power_v[:, :half], power_v[:, half:]]

    everything = all_v.at[pl.ds(0, (n - 1) * rows)]
    pltpu.make_async_copy(everything, everything, recv_sem).wait()

    def sort(b):
        block = all_v[pl.ds(pl.multiple_of(b * size, size), size), :]
        y = jnp.dot(order, block, preferred_element_type=jnp.float32)
        to = pl.ds(pl.multiple_of(b * span, span), span)
        for q in range(4):
            field_v[q, to, :] = y[q * span:(q + 1) * span, :half].astype(jnp.bfloat16)
        o = y[:, half:]
        gap_v[to, :] = o[:span] + o[span:2 * span] + o[2 * span:3 * span]
        c = o[3 * span:]
        total = jnp.zeros(c.shape, jnp.float32)
        for level in range(1, CLASSES):
            total = jnp.where(c == float(level), weight_s[level], total)
        row_ids = b * span + lax.broadcasted_iota(jnp.int32, c.shape, 0)
        col_ids = lax.broadcasted_iota(jnp.int32, c.shape, 1) % stations
        pair_v[to, :] = jnp.where(row_ids == col_ids, 0.0, total)

    each(0, n // group, sort)

    real, imag = (field_v[0], field_v[2]), (field_v[1], field_v[3])
    right = [
        jnp.concatenate([real[0], imag[0]], axis=0), jnp.concatenate([real[1], imag[1]], axis=0),
        jnp.concatenate([imag[0], -real[0]], axis=0), jnp.concatenate([imag[1], -real[1]], axis=0),
    ]
    right_real = jnp.concatenate([real[0], real[1], imag[0], imag[1]], axis=1)
    right_imag = jnp.concatenate([imag[0], imag[1], -real[0], -real[1]], axis=1)
    rights = jnp.concatenate([right_real, right_imag], axis=0)

    def correlate(b):
        to = pl.ds(pl.multiple_of(b * span, span), span)
        left = jnp.concatenate(
            [
                (power[h] * field_v[2 * h + part, to, :].astype(jnp.float32)).astype(jnp.bfloat16)
                for part in range(2) for h in range(2)
            ],
            axis=1,
        )
        part_v[to, :] = lax.dot_general(left, rights, (((1,), (1,)), ((), ())), preferred_element_type=jnp.float32)

    each(0, n // group, correlate)

    def exchange(i):
        return pltpu.make_async_remote_copy(
            src_ref=part_v, dst_ref=recv_v.at[i - 1], send_sem=pt_send.at[i - 1], recv_sem=pt_recv.at[i - 1],
            device_id={"sta": me, "pt": lax.rem(mine + i, m)}, device_id_type=MESH,
        )

    copies = [exchange(i) for i in range(1, m)]
    for copy in copies:
        copy.start()
    for copy in copies:
        copy.wait_recv()
    for copy in copies:
        copy.wait_send()

    scale = 1.0 / math.sqrt(pts * m)

    def adjoint(b, totals):
        to = pl.ds(pl.multiple_of(b * span, span), span)
        corr = part_v[to, :]
        for i in range(m - 1):
            corr = corr + recv_v[i, to, :]
        corr = corr * scale
        part_v[to, :] = corr
        a = (pair_v[to, :] * (corr - gap_v[to, :])).astype(jnp.bfloat16)
        out = []
        for h in range(2):
            field_real = jnp.dot(a, right[h], preferred_element_type=jnp.float32)
            field_imag = jnp.dot(a, right[2 + h], preferred_element_type=jnp.float32)
            term = (
                field_v[2 * h, to, :].astype(jnp.float32) * field_real
                + field_v[2 * h + 1, to, :].astype(jnp.float32) * field_imag
            )
            out.append(totals[h] + jnp.sum(term, axis=0, keepdims=True))
        return tuple(out)

    zero = jnp.zeros((1, half), jnp.float32)
    if n == group:
        totals = adjoint(0, (zero, zero))
    else:
        totals = lax.fori_loop(0, n // group, adjoint, (zero, zero))
    for h in range(2):
        grad_ref[:, h * half:(h + 1) * half] = totals[h] / stations

    share = stations // m
    tile = max(8, own)
    shared = part_v[pl.ds(pl.multiple_of(me * own // tile * tile, tile), tile), :]
    block = shared[:own]
    for i in range(1, tile // own):
        block = jnp.where(me % (tile // own) == i, shared[i * own:(i + 1) * own], block)
    for part in range(2):
        mine_of = block[:, part * stations:part * stations + share]
        for i in range(1, m):
            other = block[:, part * stations + i * share:part * stations + (i + 1) * share]
            mine_of = jnp.where(mine == i, other, mine_of)
        corr_ref[part] = mine_of

    sent = all_v.at[pl.ds(0, (n - 1) * rows)]
    pltpu.make_async_copy(sent, sent, send_sem).wait()


def solution(mesh):
    n, m = mesh.shape["sta"], mesh.shape["pt"]

    def body(greens, source_power, observed, pair_class, class_weight):
        own, pts = greens.shape[1], greens.shape[2]
        stations = own * n
        lanes = pts // 2 + 2 * stations
        any_space = pl.BlockSpec(memory_space=pl.ANY)
        vmem = pl.BlockSpec(memory_space=pltpu.VMEM)
        f32, bf16 = jnp.float32, jnp.bfloat16
        wide = (stations, 2 * stations)
        corr, grad = pl.pallas_call(
            functools.partial(kernel, n, m),
            out_shape=(
                jax.ShapeDtypeStruct((2, own, stations // m), f32),
                jax.ShapeDtypeStruct((1, pts), f32),
            ),
            in_specs=[any_space] * 5,
            out_specs=(vmem, vmem),
            scratch_shapes=[
                pltpu.VMEM(greens.shape, bf16),
                pltpu.VMEM((1, pts), f32),
                pltpu.VMEM(observed.shape, f32),
                pltpu.VMEM(pair_class.shape, jnp.int32),
                pltpu.SMEM(class_weight.shape, f32),
                pltpu.VMEM((n * own * 4, lanes), bf16),
                pltpu.VMEM((4, stations, pts // 2), bf16),
                pltpu.VMEM(wide, f32),
                pltpu.VMEM((m - 1,) + wide, f32),
                pltpu.VMEM(wide, f32),
                pltpu.VMEM(wide, f32),
                pltpu.SemaphoreType.DMA((5,)),
                pltpu.SemaphoreType.DMA,
                pltpu.SemaphoreType.DMA,
                pltpu.SemaphoreType.DMA((m - 1,)),
                pltpu.SemaphoreType.DMA((m - 1,)),
            ],
            compiler_params=pltpu.CompilerParams(
                collective_id=0, has_side_effects=True, vmem_limit_bytes=60 * 1024 * 1024
            ),
        )(greens, source_power[None], observed, pair_class, class_weight)
        return corr, grad[0]

    return jax.shard_map(
        body,
        mesh=mesh,
        in_specs=(P(None, "sta", "pt"), P("pt"), P(None, "sta", None), P("sta", None), P()),
        out_specs=(P(None, "sta", "pt"), P("pt")),
        check_vma=False,
    )
```

time: 93.1 us -> 15.5 us (0.17)
  blocking collectives: 82.2 us -> 0 us
  Pallas kernels: 0 us -> 12.7 us
  other arithmetic: 5.09 us -> 0 us
  local copies, waits for them, and re-layouts: 3.79 us -> 1.91 us
  matrix products: 1.02 us -> 0 us
    all_gather x1 -> x0, blocking collectives: 43.1 us -> none  [body(): shard_rows = lax.all_gather(greens, 'sta', axis=1, tiled=True)]
    psum x2 -> x0, blocking collectives: 39.2 us -> none  [the longest x1 36.6 us: body(): gradient = lax.psum(local_terms, 'sta') / all_stations]
    pallas_call x0 -> x1, Pallas kernels: none -> 12.7 us  [body(): pl.pallas_call(functools.partial(kernel, n, m), out_shape=(jax.ShapeDtype...]
    select_n x1 -> x0, other arithmetic: 4.48 us -> none  [pair_weights(): return jnp.where(row_ids == col_ids, 0.0, total)]
    slice x2 -> x0, local copies, waits for them, and re-layouts: 1.78 us -> none  [the longest x1 1.59 us: pair_weights(): total = total + jnp.where(classes == level, class_weight[level], 0.0)]
    dot_general x8 -> x0, matrix products: 1.02 us -> none  [the longest x4 0.51 us: last_dot(): lax.dot_general(left, right, (((1,), (1,)), ((), ())), preferred_element_...]
    unnamed x9 -> x6, local copies, waits for them, and re-layouts: 1.32 us -> 1.91 us
where the time goes in v1:
time: 15.5 us; the launch traced here: 15.2 us
  Pallas kernels  12.7 us (82%)
  local copies, waits for them, and re-layouts  1.91 us (12%)
  between operations  0.65 us (4%)
    pallas_call x1, Pallas kernels, body(): pl.pallas_call(functools.partial(kernel, n, m), out_shape=(jax.ShapeDtype...  12.7 us
    unnamed x6, local copies, waits for them, and re-layouts  1.91 us

profile of v1, /device:TPU:0, one launch (start us, length us, event | category | flops | bytes accessed | tf_op | source)
XLA Modules:
  0.0 15.2 jit_solution(18032495136143338420)
XLA Ops:
  0.6 12.7 %shard_map.68 = (f32[2,4,32]{2,1,0:T(4,128)}, f32[1,512]{1,0:T(1,128)}) custom-call(bf16[2,4,512]{2,1,0:T(4,128)(2,1)} %greens_ref.1, f32[1,512]{1,0:T(1,128)} %bitcast.2, f32[2,4,64]{2,1,0:T(4,128)} %observed_ref.1, s32[4,64]{1,0:T(4,128)} %class_ref.1, f32[8]{0:T(128)} %weight_ref.1), custom_call_target="tpu_custom_call" | custom-call | tf_op jit(solution)/shard_map/pallas_call | solution.py:208
  13.3 0.0 copy-start
  13.3 0.7 %copy-done = f32[2,4,32]{2,1,0:T(4,128)S(1)} copy-done((f32[2,4,32]{2,1,0:T(4,128)S(1)}, f32[2,4,32]{2,1,0:T(4,128)}, u32[]{:S(2)}) %copy-start) | copy-done | bytes 1048
  14.0 0.0 copy-start.1
  14.0 0.6 %copy.9 = f32[2,4,32]{2,1,0:T(4,128)} copy(f32[2,4,32]{2,1,0:T(4,128)S(1)} %copy-done) | data formatting | bytes 2048
  14.6 0.1 copy-done.1
  14.7 0.6 %copy.10 = f32[512]{0:T(512)} copy(f32[512]{0:T(512)S(1)} %bitcast.3) | data formatting | bytes 4096
Async XLA Ops:
  13.3 0.7 %copy-start = (f32[2,4,32]{2,1,0:T(4,128)S(1)}, f32[2,4,32]{2,1,0:T(4,128)}, u32[]{:S(2)}) copy-start(f32[2,4,32]{2,1,0:T(4,128)} %get-tuple-element.8) | copy-start | bytes 3076
  14.0 0.7 %copy-start.1 = (f32[1,512]{1,0:T(1,128)S(1)}, f32[1,512]{1,0:T(1,128)}, u32[]{:S(2)}) copy-start(f32[1,512]{1,0:T(1,128)} %get-tuple-element.5) | copy-start | bytes 6148

commit v2 on v1

--- a/solution.py
+++ b/solution.py
@@ -192,6 +192,17 @@
 
     sent = all_v.at[pl.ds(0, (n - 1) * rows)]
     pltpu.make_async_copy(sent, sent, send_sem).wait()
+
+
+def hand_on(corr_ref, grad_ref, corr_out, grad_out, sems):
+    copies = [
+        pltpu.make_async_copy(corr_ref, corr_out, sems.at[0]),
+        pltpu.make_async_copy(grad_ref, grad_out, sems.at[1]),
+    ]
+    for copy in copies:
+        copy.start()
+    for copy in copies:
+        copy.wait()
 
 
 def solution(mesh):
@@ -235,6 +246,14 @@
                 collective_id=0, has_side_effects=True, vmem_limit_bytes=60 * 1024 * 1024
             ),
         )(greens, source_power[None], observed, pair_class, class_weight)
+        any_pair = (any_space, any_space)
+        corr, grad = pl.pallas_call(
+            hand_on,
+            out_shape=(jax.ShapeDtypeStruct(corr.shape, f32), jax.ShapeDtypeStruct(grad.shape, f32)),
+            in_specs=any_pair,
+            out_specs=any_pair,
+            scratch_shapes=[pltpu.SemaphoreType.DMA((2,))],
+        )(corr, grad)
         return corr, grad[0]
 
     return jax.shard_map(

time: 15.5 us -> 14.8 us (0.955)
  local copies, waits for them, and re-layouts: 1.91 us -> 0 us
  Pallas kernels: 12.7 us -> 14 us
    unnamed x6 -> x0, local copies, waits for them, and re-layouts: 1.91 us -> none
    pallas_call x0 -> x1, Pallas kernels: none -> 1.31 us  [body(): pl.pallas_call(hand_on, out_shape=(jax.ShapeDtypeStruct(corr.shape, f32),...]
where the time goes in v2:
time: 14.8 us; the launch traced here: 14.6 us
  Pallas kernels  14 us (95%)
  between operations  0.64 us (4%)
    pallas_call x1, Pallas kernels, body(): pl.pallas_call(functools.partial(kernel, n, m), out_shape=(jax.ShapeDtype...  12.7 us
    pallas_call x1, Pallas kernels, body(): pl.pallas_call(hand_on, out_shape=(jax.ShapeDtypeStruct(corr.shape, f32),...  1.31 us

profile of v2, /device:TPU:0, one launch (start us, length us, event | category | flops | bytes accessed | tf_op | source)
XLA Modules:
  0.0 14.6 jit_solution(12627205214118441814)
XLA Ops:
  0.6 12.7 %shard_map.68 = (f32[2,4,32]{2,1,0:T(4,128)}, f32[1,512]{1,0:T(1,128)}) custom-call(bf16[2,4,512]{2,1,0:T(4,128)(2,1)} %greens_ref.1, f32[1,512]{1,0:T(1,128)} %bitcast.2, f32[2,4,64]{2,1,0:T(4,128)} %observed_ref.1, s32[4,64]{1,0:T(4,128)} %class_ref.1, f32[8]{0:T(128)} %weight_ref.1), custom_call_target="tpu_custom_call" | custom-call | tf_op jit(solution)/shard_map/pallas_call | solution.py:219
  13.3 1.3 %shard_map.69 = (f32[2,4,32]{2,1,0:T(4,128)}, f32[1,512]{1,0:T(1,128)}) custom-call(f32[2,4,32]{2,1,0:T(4,128)} %get-tuple-element.6.corr_ref, f32[1,512]{1,0:T(1,128)} %get-tuple-element.7.grad_ref), custom_call_target="tpu_custom_call" | custom-call | tf_op jit(solution)/shard_map/pallas_call | solution.py:250

commit v3 on v2

--- a/solution.py
+++ b/solution.py
@@ -45,7 +45,7 @@
     barrier = pltpu.get_barrier_semaphore()
 
     def greet(i):
-        pl.semaphore_signal(barrier, inc=1, device_id={"sta": lax.rem(me + i, n), "pt": mine}, device_id_type=MESH)
+        pl.semaphore_signal(barrier, inc=1, device_id={"sta": i - 1 + jnp.where(i > me, 1, 0), "pt": mine}, device_id_type=MESH)
 
     def greet_pt(i):
         pl.semaphore_signal(barrier, inc=1, device_id={"sta": me, "pt": lax.rem(mine + i, m)}, device_id_type=MESH)
@@ -75,7 +75,7 @@
     def send(i):
         pltpu.make_async_remote_copy(
             src_ref=here, dst_ref=here, send_sem=send_sem, recv_sem=recv_sem,
-            device_id={"sta": lax.rem(me + i, n), "pt": mine}, device_id_type=MESH,
+            device_id={"sta": i - 1 + jnp.where(i > me, 1, 0), "pt": mine}, device_id_type=MESH,
         ).start()
 
     each(1, n, send)
@@ -96,11 +96,48 @@
 
     def sort(b):
         block = all_v[pl.ds(pl.multiple_of(b * size, size), size), :]
-        y = jnp.dot(order, block, preferred_element_type=jnp.float32)
+        y = jnp.dot(order, block[:, :half], preferred_element_type=jnp.float32)
         to = pl.ds(pl.multiple_of(b * span, span), span)
         for q in range(4):
-            field_v[q, to, :] = y[q * span:(q + 1) * span, :half].astype(jnp.bfloat16)
-        o = y[:, half:]
+            field_v[q, to, :] = y[q * span:(q + 1) * span].astype(jnp.bfloat16)
+
+    each(0, n // group, sort)
+
+    real, imag = (field_v[0], field_v[2]), (field_v[1], field_v[3])
+    right = [
+        jnp.concatenate([real[0], imag[0]], axis=0), jnp.concatenate([real[1], imag[1]], axis=0),
+        jnp.concatenate([imag[0], -real[0]], axis=0), jnp.concatenate([imag[1], -real[1]], axis=0),
+    ]
+    right_real = jnp.concatenate([real[0], real[1], imag[0], imag[1]], axis=1)
+    right_imag = jnp.concatenate([imag[0], imag[1], -real[0], -real[1]], axis=1)
+    rights = jnp.concatenate([right_real, right_imag], axis=0)
+
+    def correlate(b):
+        to = pl.ds(pl.multiple_of(b * span, span), span)
+        left = jnp.concatenate(
+            [
+                (power[h] * field_v[2 * h + part, to, :].astype(jnp.float32)).astype(jnp.bfloat16)
+                for part in range(2) for h in range(2)
+            ],
+            axis=1,
+        )
+        part_v[to, :] = lax.dot_general(left, rights, (((1,), (1,)), ((), ())), preferred_element_type=jnp.float32)
+
+    each(0, n // group, correlate)
+
+    def exchange(i):
+        return pltpu.make_async_remote_copy(
+            src_ref=part_v, dst_ref=recv_v.at[i - 1], send_sem=pt_send.at[i - 1], recv_sem=pt_recv.at[i - 1],
+            device_id={"sta": me, "pt": lax.rem(mine + i, m)}, device_id_type=MESH,
+        )
+
+    copies = [exchange(i) for i in range(1, m)]
+    for copy in copies:
+        copy.start()
+    def sort_side(b):
+        block = all_v[pl.ds(pl.multiple_of(b * size, size), size), half:]
+        o = jnp.dot(order, block, preferred_element_type=jnp.float32)
+        to = pl.ds(pl.multiple_of(b * span, span), span)
         gap_v[to, :] = o[:span] + o[span:2 * span] + o[2 * span:3 * span]
         c = o[3 * span:]
         total = jnp.zeros(c.shape, jnp.float32)
@@ -110,43 +147,10 @@
         col_ids = lax.broadcasted_iota(jnp.int32, c.shape, 1) % stations
         pair_v[to, :] = jnp.where(row_ids == col_ids, 0.0, total)
 
-    each(0, n // group, sort)
-
-    real, imag = (field_v[0], field_v[2]), (field_v[1], field_v[3])
-    right = [
-        jnp.concatenate([real[0], imag[0]], axis=0), jnp.concatenate([real[1], imag[1]], axis=0),
-        jnp.concatenate([imag[0], -real[0]], axis=0), jnp.concatenate([imag[1], -real[1]], axis=0),
-    ]
-    right_real = jnp.concatenate([real[0], real[1], imag[0], imag[1]], axis=1)
-    right_imag = jnp.concatenate([imag[0], imag[1], -real[0], -real[1]], axis=1)
-    rights = jnp.concatenate([right_real, right_imag], axis=0)
-
-    def correlate(b):
-        to = pl.ds(pl.multiple_of(b * span, span), span)
-        left = jnp.concatenate(
-            [
-                (power[h] * field_v[2 * h + part, to, :].astype(jnp.float32)).astype(jnp.bfloat16)
-                for part in range(2) for h in range(2)
-            ],
-            axis=1,
-        )
-        part_v[to, :] = lax.dot_general(left, rights, (((1,), (1,)), ((), ())), preferred_element_type=jnp.float32)
-
-    each(0, n // group, correlate)
-
-    def exchange(i):
-        return pltpu.make_async_remote_copy(
-            src_ref=part_v, dst_ref=recv_v.at[i - 1], send_sem=pt_send.at[i - 1], recv_sem=pt_recv.at[i - 1],
-            device_id={"sta": me, "pt": lax.rem(mine + i, m)}, device_id_type=MESH,
-        )
-
-    copies = [exchange(i) for i in range(1, m)]
-    for copy in copies:
-        copy.start()
+    each(0, n // group, sort_side)
+
     for copy in copies:
         copy.wait_recv()
-    for copy in copies:
-        copy.wait_send()
 
     scale = 1.0 / math.sqrt(pts * m)
 
@@ -156,8 +160,8 @@
         for i in range(m - 1):
             corr = corr + recv_v[i, to, :]
         corr = corr * scale
-        part_v[to, :] = corr
         a = (pair_v[to, :] * (corr - gap_v[to, :])).astype(jnp.bfloat16)
+        gap_v[to, :] = corr
         out = []
         for h in range(2):
             field_real = jnp.dot(a, right[h], preferred_element_type=jnp.float32)
@@ -179,7 +183,7 @@
 
     share = stations // m
     tile = max(8, own)
-    shared = part_v[pl.ds(pl.multiple_of(me * own // tile * tile, tile), tile), :]
+    shared = gap_v[pl.ds(pl.multiple_of(me * own // tile * tile, tile), tile), :]
     block = shared[:own]
     for i in range(1, tile // own):
         block = jnp.where(me % (tile // own) == i, shared[i * own:(i + 1) * own], block)
@@ -190,6 +194,8 @@
             mine_of = jnp.where(mine == i, other, mine_of)
         corr_ref[part] = mine_of
 
+    for copy in copies:
+        copy.wait_send()
     sent = all_v.at[pl.ds(0, (n - 1) * rows)]
     pltpu.make_async_copy(sent, sent, send_sem).wait()
 

time: 14.8 us -> 14.7 us (level)
  the two profiles are of different devices: /device:TPU:0 before, /device:TPU:1 now
where the time goes in v3:
time: 14.7 us; the launch traced here: 14.5 us
  Pallas kernels  13.8 us (94%)
  between operations  0.64 us (4%)
    pallas_call x1, Pallas kernels, body(): pl.pallas_call(functools.partial(kernel, n, m), out_shape=(jax.ShapeDtype...  12.5 us
    pallas_call x1, Pallas kernels, body(): pl.pallas_call(hand_on, out_shape=(jax.ShapeDtypeStruct(corr.shape, f32),...  1.31 us

profile of v3, /device:TPU:1, one launch (start us, length us, event | category | flops | bytes accessed | tf_op | source)
XLA Modules:
  0.0 14.5 jit_solution(5492799917176592406)
XLA Ops:
  0.6 12.5 %shard_map.68 = (f32[2,4,32]{2,1,0:T(4,128)}, f32[1,512]{1,0:T(1,128)}) custom-call(bf16[2,4,512]{2,1,0:T(4,128)(2,1)} %greens_ref.1, f32[1,512]{1,0:T(1,128)} %bitcast.2, f32[2,4,64]{2,1,0:T(4,128)} %observed_ref.1, s32[4,64]{1,0:T(4,128)} %class_ref.1, f32[8]{0:T(128)} %weight_ref.1), custom_call_target="tpu_custom_call" | custom-call | tf_op jit(solution)/shard_map/pallas_call | solution.py:225
  13.2 1.3 %shard_map.69 = (f32[2,4,32]{2,1,0:T(4,128)}, f32[1,512]{1,0:T(1,128)}) custom-call(f32[2,4,32]{2,1,0:T(4,128)} %get-tuple-element.6.corr_ref, f32[1,512]{1,0:T(1,128)} %get-tuple-element.7.grad_ref), custom_call_target="tpu_custom_call" | custom-call | tf_op jit(solution)/shard_map/pallas_call | solution.py:256
